TPU v7x, 256 devices: a whole 4x4x8 slice. The times are simulated.
256 devices in a mesh: group: 8 (over x, core), sub: 32 (over y, z).
Axes of the slice: x: 4, y: 4, z: 8, core: 2. Of those that a mesh axis runs over, the one named last changes fastest.
Arguments:
- resid_iface: float32 [256, 16, 4352], P(('group', 'sub')), may hold values from -6 to 6
- resid_inner: float32 [256, 16, 3072], P(('group', 'sub')), may hold values from -6 to 6
- weights: float32 [256, 4352], P(('group', 'sub')), may hold values from 0.25 to 0.75
- nbr: int32 [256, 32], P(('group', 'sub')), may hold values from 0 to 1, as said below
- own2: int32 [256, 128], P(('group', 'sub')), may hold values from 0 to 2047
- cidx: int32 [256, 8], P(('group', 'sub')), may hold values from 0 to 16
- neumann: bfloat16 [256, 17, 256, 256], P(('group', 'sub'))
- dirichlet: bfloat16 [256, 8, 384, 384], P(('group', 'sub'))
- coupling: bfloat16 [256, 8, 256, 384], P(('group', 'sub')), may hold values from -0.375 to 0.375
- coarse_basis: bfloat16 [256, 4352, 128], P(('group', 'sub')), may hold values from -0.5 to 0.5
- group_basis: float32 [16384, 512], P(('group', 'sub')), may hold values from -0.25 to 0.25
- group_inverse: float32 [16384, 2048], P('group', 'sub'), as said below
- top_inverse: float32 [512, 512], replicated, as said below
Outputs:
- interface_out: float32 [256, 16, 4352], P(('group', 'sub'))
- interior_out: float32 [256, 16, 3072], P(('group', 'sub'))
Inputs may be any that keep to these rules, and one draw needn't show every extreme that they name: Symmetric within each group (nbr[(g, q), j] = nbr[(g, j), q]) with nbr[(g, q), q] = 0. `group_inverse`: each matrix of a group is symmetric. `top_inverse`: symmetric.
All inputs are finite; a program needn't handle non-finite values.
Results may differ from a plain program's by a relative error of at most 0.013.
Values may be sent and summed in bfloat16 or wider, within the bound.
A program may use at most 64 MiB of HBM per device.

v0:
```python
import jax
import jax.numpy as jnp
from jax import lax
from jax.sharding import PartitionSpec as P


def padded_2(cells, sides, width):
    for axis, dim in sides:
        count = lax.axis_size(axis)
        ends = count - 1
        head = lax.slice_in_dim(cells, 0, width, axis=dim)
        tail = lax.slice_in_dim(cells, cells.shape[dim] - width, cells.shape[dim], axis=dim)
        cells = jnp.concatenate(
            [
                lax.ppermute(tail, axis, [(i, (i + 1) % count) for i in range(ends)]),
                cells,
                lax.ppermute(head, axis, [((i + 1) % count, i) for i in range(ends)]),
            ],
            axis=dim,
        )
    return cells


def shards(
    resid_iface,
    resid_inner,
    weights,
    nbr,
    own2,
    cidx,
    neumann,
    dirichlet,
    coupling,
    coarse_basis,
    group_basis,
    group_inverse,
    top_inverse,
):
    highest = lax.Precision.HIGHEST
    nsub = lax.axis_size("sub")
    mine = lax.axis_index("sub")
    rows = resid_iface.shape[1]
    width = resid_iface.shape[2]
    slot_width = width // (nsub + 2)
    block_count = neumann.shape[1]
    block_width = neumann.shape[2]
    inner_count = dirichlet.shape[1]
    inner_width = dirichlet.shape[2]
    group_width = group_inverse.shape[0]
    share = group_inverse.shape[1]
    slot_mask = jnp.concatenate([nbr[0].astype(jnp.float32), jnp.ones((2,), jnp.float32)])
    scale = jnp.repeat(slot_mask, slot_width) * weights[0]
    weighted = (scale[None, :] * resid_iface[0]).astype(jnp.bfloat16)
    local0 = jnp.dot(weighted, coarse_basis[0], preferred_element_type=jnp.float32)
    onehot = (own2[0][:, None] == jnp.arange(group_width, dtype=jnp.int32)[None, :]).astype(
        jnp.float32
    )
    contrib = jnp.dot(local0, onehot, precision=highest)
    level2 = lax.psum(contrib.astype(jnp.bfloat16), "sub").astype(jnp.float32)
    level2_mine = lax.dynamic_slice_in_dim(level2, mine * share, share, 1)
    neumann_part = jnp.einsum(
        "rkb,kbc->rkc",
        weighted.reshape(rows, block_count, block_width),
        neumann[0],
        preferred_element_type=jnp.float32,
    ).reshape(rows, width)
    top_term = jnp.dot(level2_mine, group_basis, precision=highest)
    level3 = lax.psum(top_term, ("group", "sub"))
    coarse3 = jnp.dot(level3, top_inverse, precision=highest)
    lifted = lax.dot_general(coarse3, group_basis, (((1,), (1,)), ((), ())), precision=highest)
    coarse2_mine = jnp.dot(level2, group_inverse, precision=highest) + lifted
    coarse2 = lax.all_gather(coarse2_mine.astype(jnp.bfloat16), "sub", axis=1, tiled=True)
    values = jnp.take(coarse2, own2[0], axis=1)
    spread = lax.dot_general(
        values, coarse_basis[0], (((1,), (1,)), ((), ())), preferred_element_type=jnp.float32
    )
    scaled = scale[None, :] * (neumann_part + spread)
    slots = scaled.reshape(rows, nsub + 2, slot_width)
    received = lax.all_to_all(
        slots[:, :nsub, :].astype(jnp.bfloat16), "sub", split_axis=1, concat_axis=1, tiled=True
    ).astype(jnp.float32)
    padded = padded_2(slots[:, nsub:, :], (("group", 1),), 1)
    lower_face = slots[:, nsub, :] + padded[:, 0, :]
    upper_face = slots[:, nsub + 1, :] + padded[:, 3, :]
    total = jnp.concatenate(
        [slots[:, :nsub, :] + received, lower_face[:, None, :], upper_face[:, None, :]], axis=1
    )
    interface_out = total.reshape(rows, width)
    iface_blocks = interface_out.reshape(rows, block_count, block_width).astype(jnp.bfloat16)
    picked = jnp.take(iface_blocks, cidx[0], axis=1)
    pushed = jnp.einsum("rkb,kbc->rkc", picked, coupling[0], preferred_element_type=jnp.float32)
    inner_rhs = (resid_inner[0].reshape(rows, inner_count, inner_width) - pushed).astype(
        jnp.bfloat16
    )
    interior_out = jnp.einsum(
        "rkb,kbc->rkc", inner_rhs, dirichlet[0], preferred_element_type=jnp.float32
    ).reshape(rows, inner_count * inner_width)
    return (interface_out[None], interior_out[None])


def solution(mesh):
    placed = (
        P(("group", "sub"), None, None),
        P(("group", "sub"), None, None),
        P(("group", "sub"), None),
        P(("group", "sub"), None),
        P(("group", "sub"), None),
        P(("group", "sub"), None),
        P(("group", "sub"), None, None, None),
        P(("group", "sub"), None, None, None),
        P(("group", "sub"), None, None, None),
        P(("group", "sub"), None, None),
        P(("group", "sub"), None),
        P("group", "sub"),
        P(),
    )
    return jax.shard_map(
        shards,
        mesh=mesh,
        in_specs=placed,
        out_specs=(P(("group", "sub"), None, None), P(("group", "sub"), None, None)),
        check_vma=False,
    )
```

profile of v0, /device:TPU:1, one launch (start us, length us, event | category | flops | bytes accessed | tf_op | source)
XLA Modules:
  0.0 318.7 jit_solution(4623421728509135453)
XLA Ops:
  7.2 0.0 copy-start
  7.2 0.0 copy-start.2
  7.2 0.0 copy-start.4
  7.2 0.0 copy-start.5
  7.2 0.0 all-reduce.3.cloned.1.call-start
  7.3 0.8 convert_bitcast_fusion
  8.1 0.1 broadcast_bitcast_fusion
  8.1 0.8 fusion.45
  8.9 1.6 fusion.25
  10.5 1.8 convolution_convert_fusion
  12.3 0.0 all-reduce.3.cloned.1.call-update
  12.4 0.0 copy-done.4
  12.4 0.0 copy-done.2
  12.5 0.0 copy-done.5
  12.6 2.0 fusion.7
  14.6 0.7 copy.43
  15.3 0.0 copy-start.1
  15.3 136.0 %all-reduce.3.cloned.1.call-done = bf16[16,2048]{1,0:T(8,128)(2,1)} async-done(((bf16[16,2048]{1,0:T(8,128)(2,1)}), bf16[16,2048]{1,0:T(8,128)(2,1)}) %all-reduce.3.cloned.1.call-update) | async-done | bytes 65552 | tf_op jit(solution)/shard_map/psum | solution.py:59
  151.3 1.7 fusion.47
  153.0 78.0 %psum.15 = f32[16,512]{1,0:T(8,128)S(1)} all-reduce(f32[16,512]{1,0:T(8,128)} %fusion.47), channel_id=1, replica_groups=mesh['group'=8,'sub'=32] {'group','sub'}, use_global_device_ids=true, to_apply=%region_1.0 | all-reduce | flops 8192 | bytes 65536 | tf_op jit(solution)/shard_map/psum | solution.py:68
  231.1 0.0 copy-start.3
  231.1 1.9 fusion.58
  233.0 1.4 fusion.57
  234.4 0.0 copy-done.3
  234.4 0.2 fusion.28
  234.6 35.0 %all-gather = bf16[32,64,16]{1,2,0:T(8,128)(2,1)} all-gather(bf16[1,64,16]{1,2,0:T(8,128)(2,1)S(1)} %fusion.28), channel_id=1, replica_groups=mesh['group'=8,'sub'=32] {'sub'}, dimensions={0}, use_global_device_ids=true | all-gather | bytes 67584 | tf_op jit(solution)/shard_map/all_gather | solution.py:72
  269.6 1.9 copy.41
  271.5 1.8 gather_fusion
  273.3 0.0 copy-done.1
  273.3 2.2 fusion
  275.5 1.0 reshape.101
  276.5 12.7 %collective-permute-start = (f32[16,1,128]{2,1,0:T(1,128)S(1)}, f32[16,1,128]{2,1,0:T(1,128)S(1)}, u32[]{:S(2)}, u32[]{:S(2)}) collective-permute-start(f32[16,1,128]{2,1,0:T(1,128)S(1)} %get-tuple-element.4), channel_id=1, source_target_pairs={{0,32},{32,64},{64,96},{96,128},{128,160},{160,192},{192,224},{1,3... | collective-permute-start | bytes 24584 | tf_op jit(solution)/shard_map/ppermute | solution.py:15
  289.2 1.9 collective-permute-start.1
  291.2 0.7 copy.36
  291.9 5.6 %all-to-all-start = ((bf16[16,32,128]{2,0,1:T(8,128)(2,1)}), bf16[16,32,128]{2,0,1:T(8,128)(2,1)S(1)}, u32[]{:S(2)}, u32[]{:S(2)}) async-start(bf16[16,32,128]{2,0,1:T(8,128)(2,1)} %copy.36), calls=%async_computation | async-start | bytes 262144 | tf_op jit(solution)/shard_map/all_to_all | solution.py:79
  297.5 1.0 copy.45
  298.5 0.0 collective-permute-done
  298.5 0.0 collective-permute-done.1
  298.6 8.8 %all-to-all-done = bf16[16,32,128]{2,0,1:T(8,128)(2,1)S(1)} async-done(((bf16[16,32,128]{2,0,1:T(8,128)(2,1)}), bf16[16,32,128]{2,0,1:T(8,128)(2,1)S(1)}, u32[]{:S(2)}, u32[]{:S(2)}) %all-to-all-start) | async-done | bytes 131104 | tf_op jit(solution)/shard_map/all_to_all | solution.py:79
  307.5 0.1 convert_element_type.48
  307.6 0.6 gather_fusion.1
  308.2 0.0 copy-done
  308.2 2.1 fusion.10
  310.3 0.1 copy.40
  310.4 0.7 broadcast_in_dim_reshape.7
  311.1 0.8 broadcast_in_dim_reshape.6
  (17 shorter events, 0.3 us)
Async XLA Ops:
  7.2 301.0 %copy-start = (bf16[1,8,384,384]{3,2,1,0:T(8,128)(2,1)S(1)}, bf16[1,8,384,384]{3,2,1,0:T(8,128)(2,1)}, u32[]{:S(2)}) copy-start(bf16[1,8,384,384]{3,2,1,0:T(8,128)(2,1)} %param.20) | copy-start | bytes 7077892
  7.2 5.2 %copy-start.2 = (f32[1,16,4352]{2,1,0:T(8,128)S(1)}, f32[1,16,4352]{2,1,0:T(8,128)}, u32[]{:S(2)}) copy-start(f32[1,16,4352]{2,1,0:T(8,128)} %param.13) | copy-start | bytes 835588
  7.2 5.2 %copy-start.4 = (s32[1,128]{1,0:T(1,128)S(1)}, s32[1,128]{1,0:T(1,128)}, u32[]{:S(2)}) copy-start(s32[1,128]{1,0:T(1,128)} %param.17) | copy-start | bytes 1540
  7.2 5.3 %copy-start.5 = (s32[1,8]{1,0:T(1,128)S(1)}, s32[1,8]{1,0:T(1,128)}, u32[]{:S(2)}) copy-start(s32[1,8]{1,0:T(1,128)} %param.18) | copy-start | bytes 100
  7.2 144.1 %all-reduce.3.cloned.1.call-start = ((), (), s32[]{:S(2)}) async-start(), calls=%async_computation.1 | async-start | bytes 131072 | tf_op jit(solution)/shard_map/psum | solution.py:59
  15.3 257.9 %copy-start.1 = (bf16[1,4352,128]{2,1,0:T(8,128)(2,1)S(1)}, bf16[1,4352,128]{2,1,0:T(8,128)(2,1)}, u32[]{:S(2)}) copy-start(bf16[1,4352,128]{2,1,0:T(8,128)(2,1)} %param.22) | copy-start | bytes 3342340
  231.1 3.3 %copy-start.3 = (f32[64,512]{1,0:T(8,128)S(1)}, f32[64,512]{1,0:T(8,128)}, u32[]{:S(2)}) copy-start(f32[64,512]{1,0:T(8,128)} %param.23) | copy-start | bytes 393220
  276.5 22.0 %collective-permute-start = (f32[16,1,128]{2,1,0:T(1,128)S(1)}, f32[16,1,128]{2,1,0:T(1,128)S(1)}, u32[]{:S(2)}, u32[]{:S(2)}) collective-permute-start(f32[16,1,128]{2,1,0:T(1,128)S(1)} %get-tuple-element.4), channel_id=1, source_target_pairs={{0,32},{32,64},{64,96},{96,128},{128,160},{160,192},{192,224},{1,3... | collective-permute-start | bytes 24584 | tf_op jit(solution)/shard_map/ppermute | solution.py:15
  289.2 9.3 %collective-permute-start.1 = (f32[16,1,128]{2,1,0:T(1,128)S(1)}, f32[16,1,128]{2,1,0:T(1,128)S(1)}, u32[]{:S(2)}, u32[]{:S(2)}) collective-permute-start(f32[16,1,128]{2,1,0:T(1,128)S(1)} %get-tuple-element.5), channel_id=1, source_target_pairs={{32,0},{64,32},{96,64},{128,96},{160,128},{192,160},{224,192},{33,... | collective-permute-start | bytes 24584 | tf_op jit(solution)/shard_map/ppermute | solution.py:17
  291.9 15.5 %all-to-all-start = ((bf16[16,32,128]{2,0,1:T(8,128)(2,1)}), bf16[16,32,128]{2,0,1:T(8,128)(2,1)S(1)}, u32[]{:S(2)}, u32[]{:S(2)}) async-start(bf16[16,32,128]{2,0,1:T(8,128)(2,1)} %copy.36), calls=%async_computation | async-start | bytes 262144 | tf_op jit(solution)/shard_map/all_to_all | solution.py:79
Sparse Core Ops, SparseCore 0:
  12.5 138.7 all-reduce.2
where the time goes:
time: 319 us
  waiting for transfers between devices  145 us (45%)
  blocking collectives  113 us (35%)
  starting transfers between devices  20.3 us (6%)
  matrix products  15 us (5%)
  between operations  14.3 us (4%)
  local copies, waits for them, and re-layouts  9.48 us (3%)
    psum x1, waiting for transfers between devices, shards(): level2 = lax.psum(contrib.astype(jnp.bfloat16), 'sub').astype(jnp.float32)  136 us
    psum x1, blocking collectives, shards(): level3 = lax.psum(top_term, ('group', 'sub'))  78 us
    all_gather x1, blocking collectives, shards(): lax.all_gather(coarse2_mine.astype(jnp.bfloat16), 'sub', axis=1, tiled=True)  35 us
    ppermute x1, starting transfers between devices, padded_2(): lax.ppermute(tail, axis, [(i, (i + 1) % count) for i in range(ends)])  12.7 us
    all_to_all x1, waiting for transfers between devices, shards(): lax.all_to_all(slots[:, :nsub, :].astype(jnp.bfloat16), 'sub', split_axis...  8.85 us
  transfers between devices with their start and end apart: 4, of which 2 were waited for; matrix products, arithmetic and copies ran while one was open for 1% of the time, Pallas kernels for 0%

commit v1 on v0

--- a/solution.py
+++ b/solution.py
@@ -1,7 +1,16 @@
+import functools
 import jax
 import jax.numpy as jnp
 from jax import lax
 from jax.sharding import PartitionSpec as P
+
+
+def _balance_rates(vals, comm_axis):
+    step_out = jnp.sum(jax.lax.all_gather(vals, axis_name=comm_axis), 0)
+    return step_out
+
+
+_prepare_area = functools.partial(_balance_rates, comm_axis="sub")
 
 
 def padded_2(cells, sides, width):
@@ -56,7 +65,7 @@
         jnp.float32
     )
     contrib = jnp.dot(local0, onehot, precision=highest)
-    level2 = lax.psum(contrib.astype(jnp.bfloat16), "sub").astype(jnp.float32)
+    level2 = _prepare_area(contrib.astype(jnp.bfloat16)).astype(jnp.float32)
     level2_mine = lax.dynamic_slice_in_dim(level2, mine * share, share, 1)
     neumann_part = jnp.einsum(
         "rkb,kbc->rkc",

time: 319 us -> 261 us (0.82)
  waiting for transfers between devices: 145 us -> 83.9 us
    psum x1 -> x0, waiting for transfers between devices: 136 us -> none  [shards(): level2 = lax.psum(contrib.astype(jnp.bfloat16), 'sub').astype(jnp.float32)]
    all_gather x0 -> x1, waiting for transfers between devices: none -> 75 us  [_balance_rates(): step_out = jnp.sum(jax.lax.all_gather(vals, axis_name=comm_axis), 0)]
  transfers between devices with their start and end apart: 4 -> 4, of which waited for: 2 -> 2; matrix products, arithmetic and copies ran while one was open for 1% -> 2% of each run, Pallas kernels for 0% -> 0%
where the time goes in v1:
time: 261 us; the launch traced here: 260 us
  blocking collectives  113 us (43%)
  waiting for transfers between devices  83.9 us (32%)
  starting transfers between devices  20.2 us (8%)
  matrix products  15.1 us (6%)
  between operations  14.3 us (5%)
  local copies, waits for them, and re-layouts  9.47 us (4%)
  other arithmetic  4.37 us (2%)
    psum x1, blocking collectives, shards(): level3 = lax.psum(top_term, ('group', 'sub'))  78.2 us
    all_gather x1, waiting for transfers between devices, _balance_rates(): step_out = jnp.sum(jax.lax.all_gather(vals, axis_name=comm_axis), 0)  75 us
    all_gather x1, blocking collectives, shards(): lax.all_gather(coarse2_mine.astype(jnp.bfloat16), 'sub', axis=1, tiled=True)  34.4 us
    ppermute x1, starting transfers between devices, padded_2(): lax.ppermute(tail, axis, [(i, (i + 1) % count) for i in range(ends)])  12.5 us
    all_to_all x1, waiting for transfers between devices, shards(): lax.all_to_all(slots[:, :nsub, :].astype(jnp.bfloat16), 'sub', split_axis...  8.86 us
    all_to_all x1, starting transfers between devices, shards(): lax.all_to_all(slots[:, :nsub, :].astype(jnp.bfloat16), 'sub', split_axis...  5.8 us
  transfers between devices with their start and end apart: 4, of which 2 were waited for; matrix products, arithmetic and copies ran while one was open for 2% of the time, Pallas kernels for 0%

profile of v1, /device:TPU:1, one launch (start us, length us, event | category | flops | bytes accessed | tf_op | source)
XLA Modules:
  0.0 259.9 jit_solution(10569810040552177556)
XLA Ops:
  7.2 0.0 copy-start
  7.2 0.0 copy-start.2
  7.2 0.0 all-gather.4.cloned.1.call-start
  7.2 0.8 convert_bitcast_fusion
  8.1 0.1 broadcast_bitcast_fusion
  8.2 0.8 fusion.45
  8.9 1.6 fusion.25
  10.5 1.8 convolution_convert_fusion
  12.3 0.0 all-gather.4.cloned.1.call-update
  12.4 0.0 copy-done.2
  12.5 0.0 copy-start.4
  12.5 0.0 copy-start.5
  12.5 2.0 fusion.7
  14.6 0.7 copy.43
  15.3 0.0 copy-done.4
  15.3 0.0 copy-done.5
  15.4 75.0 %all-gather.4.cloned.1.call-done = bf16[512,2048]{1,0:T(8,128)(2,1)} async-done(((bf16[16,2048]{1,0:T(8,128)(2,1)}), bf16[512,2048]{1,0:T(8,128)(2,1)}) %all-gather.4.cloned.1.call-update) | async-done | bytes 2097168 | tf_op jit(solution)/shard_map/all_gather | solution.py:9
  90.4 2.6 reduce_sum.12
  92.9 0.0 copy-start.1
  92.9 1.8 fusion.47
  94.8 78.2 %psum.7 = f32[16,512]{1,0:T(8,128)S(1)} all-reduce(f32[16,512]{1,0:T(8,128)} %fusion.47), channel_id=1, replica_groups=mesh['group'=8,'sub'=32] {'group','sub'}, use_global_device_ids=true, to_apply=%region_1.0 | all-reduce | flops 8192 | bytes 65536 | tf_op jit(solution)/shard_map/psum | solution.py:77
  172.9 0.0 copy-start.3
  172.9 1.5 fusion.57
  174.4 1.9 fusion.58
  176.2 0.0 copy-done.3
  176.2 0.2 fusion.28
  176.5 34.4 %all-gather.1 = bf16[32,64,16]{1,2,0:T(8,128)(2,1)} all-gather(bf16[1,64,16]{1,2,0:T(8,128)(2,1)S(1)} %fusion.28), channel_id=1, replica_groups=mesh['group'=8,'sub'=32] {'sub'}, dimensions={0}, use_global_device_ids=true | all-gather | bytes 67584 | tf_op jit(solution)/shard_map/all_gather | solution.py:81
  210.9 1.9 copy.41
  212.8 1.8 gather_fusion
  214.6 0.0 copy-done.1
  214.6 2.2 fusion
  216.8 1.0 reshape.101
  217.8 12.5 %collective-permute-start = (f32[16,1,128]{2,1,0:T(1,128)S(1)}, f32[16,1,128]{2,1,0:T(1,128)S(1)}, u32[]{:S(2)}, u32[]{:S(2)}) collective-permute-start(f32[16,1,128]{2,1,0:T(1,128)S(1)} %get-tuple-element.4), channel_id=1, source_target_pairs={{0,32},{32,64},{64,96},{96,128},{128,160},{160,192},{192,224},{1,3... | collective-permute-start | bytes 24584 | tf_op jit(solution)/shard_map/ppermute | solution.py:24
  230.3 1.9 collective-permute-start.1
  232.2 0.7 copy.36
  232.9 5.8 %all-to-all-start = ((bf16[16,32,128]{2,0,1:T(8,128)(2,1)}), bf16[16,32,128]{2,0,1:T(8,128)(2,1)S(1)}, u32[]{:S(2)}, u32[]{:S(2)}) async-start(bf16[16,32,128]{2,0,1:T(8,128)(2,1)} %copy.36), calls=%async_computation | async-start | bytes 262144 | tf_op jit(solution)/shard_map/all_to_all | solution.py:88
  238.7 1.0 copy.45
  239.7 0.0 collective-permute-done
  239.7 0.0 collective-permute-done.1
  239.8 8.9 %all-to-all-done = bf16[16,32,128]{2,0,1:T(8,128)(2,1)S(1)} async-done(((bf16[16,32,128]{2,0,1:T(8,128)(2,1)}), bf16[16,32,128]{2,0,1:T(8,128)(2,1)S(1)}, u32[]{:S(2)}, u32[]{:S(2)}) %all-to-all-start) | async-done | bytes 131104 | tf_op jit(solution)/shard_map/all_to_all | solution.py:88
  248.8 0.1 convert_element_type.50
  248.8 0.6 gather_fusion.1
  249.4 0.0 copy-done
  249.4 2.1 fusion.10
  251.5 0.1 copy.40
  251.6 0.7 broadcast_in_dim_reshape.7
  252.3 0.8 broadcast_in_dim_reshape.6
  (17 shorter events, 0.3 us)
Async XLA Ops:
  7.2 242.2 %copy-start = (bf16[1,8,384,384]{3,2,1,0:T(8,128)(2,1)S(1)}, bf16[1,8,384,384]{3,2,1,0:T(8,128)(2,1)}, u32[]{:S(2)}) copy-start(bf16[1,8,384,384]{3,2,1,0:T(8,128)(2,1)} %param.20) | copy-start | bytes 7077892
  7.2 5.2 %copy-start.2 = (f32[1,16,4352]{2,1,0:T(8,128)S(1)}, f32[1,16,4352]{2,1,0:T(8,128)}, u32[]{:S(2)}) copy-start(f32[1,16,4352]{2,1,0:T(8,128)} %param.13) | copy-start | bytes 835588
  7.2 83.2 %all-gather.4.cloned.1.call-start = ((), (), s32[]{:S(2)}) async-start(), calls=%async_computation.1 | async-start | bytes 2162688 | tf_op jit(solution)/shard_map/all_gather | solution.py:9
  12.5 2.8 %copy-start.4 = (s32[1,128]{1,0:T(1,128)S(1)}, s32[1,128]{1,0:T(1,128)}, u32[]{:S(2)}) copy-start(s32[1,128]{1,0:T(1,128)} %param.17) | copy-start | bytes 1540
  12.5 2.8 %copy-start.5 = (s32[1,8]{1,0:T(1,128)S(1)}, s32[1,8]{1,0:T(1,128)}, u32[]{:S(2)}) copy-start(s32[1,8]{1,0:T(1,128)} %param.18) | copy-start | bytes 100
  92.9 121.7 %copy-start.1 = (bf16[1,4352,128]{2,1,0:T(8,128)(2,1)S(1)}, bf16[1,4352,128]{2,1,0:T(8,128)(2,1)}, u32[]{:S(2)}) copy-start(bf16[1,4352,128]{2,1,0:T(8,128)(2,1)} %param.22) | copy-start | bytes 3342340
  172.9 3.3 %copy-start.3 = (f32[64,512]{1,0:T(8,128)S(1)}, f32[64,512]{1,0:T(8,128)}, u32[]{:S(2)}) copy-start(f32[64,512]{1,0:T(8,128)} %param.23) | copy-start | bytes 393220
  217.8 21.9 %collective-permute-start = (f32[16,1,128]{2,1,0:T(1,128)S(1)}, f32[16,1,128]{2,1,0:T(1,128)S(1)}, u32[]{:S(2)}, u32[]{:S(2)}) collective-permute-start(f32[16,1,128]{2,1,0:T(1,128)S(1)} %get-tuple-element.4), channel_id=1, source_target_pairs={{0,32},{32,64},{64,96},{96,128},{128,160},{160,192},{192,224},{1,3... | collective-permute-start | bytes 24584 | tf_op jit(solution)/shard_map/ppermute | solution.py:24
  230.3 9.4 %collective-permute-start.1 = (f32[16,1,128]{2,1,0:T(1,128)S(1)}, f32[16,1,128]{2,1,0:T(1,128)S(1)}, u32[]{:S(2)}, u32[]{:S(2)}) collective-permute-start(f32[16,1,128]{2,1,0:T(1,128)S(1)} %get-tuple-element.5), channel_id=1, source_target_pairs={{32,0},{64,32},{96,64},{128,96},{160,128},{192,160},{224,192},{33,... | collective-permute-start | bytes 24584 | tf_op jit(solution)/shard_map/ppermute | solution.py:26
  232.9 15.7 %all-to-all-start = ((bf16[16,32,128]{2,0,1:T(8,128)(2,1)}), bf16[16,32,128]{2,0,1:T(8,128)(2,1)S(1)}, u32[]{:S(2)}, u32[]{:S(2)}) async-start(bf16[16,32,128]{2,0,1:T(8,128)(2,1)} %copy.36), calls=%async_computation | async-start | bytes 262144 | tf_op jit(solution)/shard_map/all_to_all | solution.py:88
Sparse Core Ops, SparseCore 0:
  12.5 77.8 all-gather.3
